TPU v7x, 512 devices: a whole 4x4x16 slice. The times are simulated.
512 devices in a mesh: site: 16 (over z), term: 32 (over y, x, core).
Axes of the slice: x: 4, y: 4, z: 16, core: 2. Of those that a mesh axis runs over, the one named last changes fastest.
Arguments:
- left_edge: float32 [128, 2, 128, 128], P('term'), as said below
- mps: float32 [64, 4, 2, 128, 128], P('site', None, None, None, 'term')
- block_list: int32 [64, 4, 2], P('site'), may hold values from 0 to 1, each once within a row
- coupling: float32 [128, 64, 4], P('term', 'site'), may hold values from 0.6 to 1.6
- right_env: float32 [16, 128, 2, 128, 128], P('site', 'term'), as said below
- start_vector: float32 [16, 2, 128, 128], P('site', None, None, 'term'), may hold values from -6 to 6
Outputs:
- env_out: float32 [16, 128, 2, 128, 128], P('site', 'term')
- state: float32 [16, 2, 128, 128], P('site', None, None, 'term')
- energy: float32 [16], P('site')
Inputs may be any that keep to these rules, and one draw needn't show every extreme that they name: Each row of block_list names every one of the 2 sectors once. Every block of left_edge is symmetric. Every block of right_env is symmetric.
All inputs are finite; a program needn't handle non-finite values.
Results may differ from a plain program's by a relative error of at most 0.0003.
Values sent between devices are 32-bit elements; how exact they have to be, the bound alone decides.
A program may use at most 64 MiB of HBM per device.

v0:
```python
import jax
import jax.numpy as jnp
from jax import lax
from jax.sharding import PartitionSpec as P

ITERS = 4


step_size = 0.5
epsilon = 1e-06


def from_behind(value, axis, steps):
    count = lax.axis_size(axis)
    leading, last = (max(0, -steps), min(count, count - steps))
    return lax.ppermute(value, axis, [(source, source + steps) for source in range(leading, last)])


def env_step(environment, blocks, sector_map, weights):
    sectors = environment.shape[1]
    onehot = (sector_map[:, :, None] == jnp.arange(sectors, dtype=jnp.int32)[None, None, :]).astype(
        jnp.float32
    )
    sourced = jnp.einsum("pts,wsij->wptij", onehot, environment, precision=lax.Precision.HIGHEST)
    left_part = jnp.einsum("wptij,ptjk->wptik", sourced, blocks, precision=lax.Precision.HIGHEST)
    sandwich = jnp.einsum("ptji,wptjk->wptik", blocks, left_part, precision=lax.Precision.HIGHEST)
    return jnp.einsum("wp,wptik->wtik", weights, sandwich, precision=lax.Precision.HIGHEST)


def body(left_edge, mps, block_list, coupling, right_env, start_vector):
    blocks = lax.all_gather(mps, "term", axis=4, tiled=True)
    segment = lax.axis_index("site")
    segments = lax.axis_size("site")
    term_count = lax.axis_size("term")
    local_terms = left_edge.shape[0]
    orbitals = blocks.shape[0]
    group_size = local_terms // 2
    group_count = local_terms // group_size

    def advance(environment, group):
        weights = lax.dynamic_slice_in_dim(coupling, group * group_size, group_size, 0)
        for within in range(orbitals):
            environment = env_step(
                environment, blocks[within], block_list[within], weights[:, within, :]
            )
        return environment

    def chain_step(moment, carry):
        outgoing, arrived, leaving = carry
        received = from_behind(outgoing, "site", 1)
        group = moment - segment
        valid = jnp.logical_and(group >= 0, group < group_count)
        group_clip = jnp.clip(group, 0, group_count - 1)
        start = group_clip * group_size
        own_edge = lax.dynamic_slice_in_dim(left_edge, start, group_size, 0)
        incoming = jnp.where(segment == 0, own_edge, received)
        produced = lax.cond(
            valid,
            lambda operands: advance(operands[0], operands[1]),
            lambda operands: jnp.zeros_like(operands[0]),
            (incoming, group_clip),
        )
        current_in = lax.dynamic_slice_in_dim(arrived, start, group_size, 0)
        arrived = lax.dynamic_update_slice_in_dim(
            arrived, jnp.where(valid, incoming, current_in), start, 0
        )
        current_out = lax.dynamic_slice_in_dim(leaving, start, group_size, 0)
        leaving = lax.dynamic_update_slice_in_dim(
            leaving, jnp.where(valid, produced, current_out), start, 0
        )
        return (produced, arrived, leaving)

    initial = (
        jnp.zeros((group_size,) + left_edge.shape[1:], jnp.float32),
        jnp.zeros_like(left_edge),
        jnp.zeros_like(left_edge),
    )
    outgoing, arrived, leaving = lax.fori_loop(0, segments + group_count - 1, chain_step, initial)
    right_side = right_env[0]
    inverse_terms = 1.0 / (local_terms * term_count)
    block_rows = left_edge.shape[2]
    entries = left_edge.shape[1] * block_rows * block_rows
    rayleigh = jnp.float32(0.0)
    vector = lax.all_gather(start_vector[0], "term", axis=2, tiled=True)
    vector = vector / jnp.sqrt(jnp.sum(vector * vector) / entries + epsilon)
    for repeat in range(ITERS):
        product = jnp.einsum("wsij,sjk->wsik", arrived, vector, precision=lax.Precision.HIGHEST)
        image = (
            lax.psum(
                jnp.einsum("wsik,wskl->sil", product, right_side, precision=lax.Precision.HIGHEST),
                "term",
            )
            * inverse_terms
        )
        rayleigh = jnp.sum(vector * image) / jnp.sum(vector * vector)
        corrected = vector - step_size * (image - rayleigh * vector)
        vector = corrected / jnp.sqrt(jnp.sum(corrected * corrected) / entries + epsilon)
    columns = block_rows // term_count
    result = lax.dynamic_slice_in_dim(vector, lax.axis_index("term") * columns, columns, 2)
    return (leaving[None], result[None], jnp.reshape(rayleigh, (1,)))


def solution(mesh):
    in_specs = (
        P("term", None, None, None),
        P("site", None, None, None, "term"),
        P("site", None, None),
        P("term", "site", None),
        P("site", "term", None, None, None),
        P("site", None, None, "term"),
    )
    out_specs = (P("site", "term", None, None, None), P("site", None, None, "term"), P("site"))
    return jax.shard_map(body, mesh=mesh, in_specs=in_specs, out_specs=out_specs, check_vma=False)
```

profile of v0, /device:TPU:481, one launch (start us, length us, event | category | flops | bytes accessed | tf_op | source)
XLA Modules:
  0.0 1699.7 jit_solution(11258564951052058227)
XLA Ops:
  10.8 25.4 %all-gather = f32[1,2,128,128]{2,1,0,3:T(2,128)S(1)} all-gather(f32[1,2,128,4]{2,1,0,3:T(2,128)S(1)} %copy.48), channel_id=2, replica_groups=mesh['site'=16,'term'=32] {'term'}, dimensions={3}, use_global_device_ids=true | all-gather | bytes 135168 | tf_op jit(solution)/shard_map/all_gather | solution.py:84
  37.7 32.7 %all-gather.3.cloned.1.call-done = f32[4,4,2,128,128]{3,1,2,0,4:T(4,128)} async-done(((f32[4,4,2,128,4]{3,1,2,0,4:T(4,128)}), f32[4,4,2,128,128]{3,1,2,0,4:T(4,128)}) %all-gather.3.cloned.1.call-update) | async-done | bytes 2097168 | tf_op jit(solution)/shard_map/all_gather | solution.py:31
  74.0 1056.2 %while.18 = (s32[]{:T(128)}, f32[2,2,128,128]{3,2,1,0:T(8,128)}, f32[4,2,128,128]{3,2,0,1:T(8,128)S(1)}, f32[4,2,128,128]{3,2,1,0:T(8,128)}, s32[]{:T(128)}, /*i...) while((s32[]{:T(128)}, f32[2,2,128,128]{3,2,1,0:T(8,128)}, ...), condition=%wide.region_3.4_spmd, body=%wide.region_0.3_spmd.sunk | while | flops 3259170816 | bytes 44569020 | solution.py:78
  75.3 8.4 collective-permute-done
  89.3 7.5 collective-permute-done
  102.4 6.6 collective-permute-done
  114.5 7.6 collective-permute-done
  127.6 6.0 collective-permute-done
  139.2 6.9 collective-permute-done
  151.7 7.2 collective-permute-done
  164.5 7.2 collective-permute-done
  177.3 7.2 collective-permute-done
  190.0 7.2 collective-permute-done
  202.8 7.2 collective-permute-done
  215.6 7.8 collective-permute-done
  228.9 9.2 collective-permute-done
  243.6 11.0 collective-permute-done
  260.2 9.8 collective-permute-done
  275.5 730.9 %collective-permute-done = f32[2,2,128,128]{3,2,1,0:T(8,128)S(1)} collective-permute-done((f32[2,2,128,128]{3,2,1,0:T(8,128)}, f32[2,2,128,128]{3,2,1,0:T(8,128)S(1)}, u32[]{:S(2)}, u32[]{:S(2)}) %collective-permute-start) | collective-permute-done | bytes 262176 | tf_op jit(solution)/shard_map/while/body/eval_jaxpr/ppermute | solution.py:16
  1008.3 51.3 %conditional.2 = (f32[2,2,128,128]{3,2,1,0:T(8,128)}) conditional(s32[]{:T(128)} %convert_element_type.13, () %tuple.62, (s32[]{:T(128)}, f32[4,4,4]{2,0,1:T(4,128)}, s32[4,4,2]{1,2,0:T(2,128)S(1)}, f32[2,2,128,128]{3,2,1,0:T(8,128)S(1)}, f32[4,4,2,128,128]{4,3,2,1,0:T(8,128)S(1)}) %tuple.63), branch_computations={%region_1.1_spmd, %region_2.2_spmd} | conditional | flops 3258974208 | bytes 39848536 | solution.py:57
  1019.5 3.0 fusion.57
  1044.1 3.0 fusion.59
  1055.8 3.7 fusion.60
  1062.6 7.2 collective-permute-done
  1071.6 51.3 %conditional.2 = (f32[2,2,128,128]{3,2,1,0:T(8,128)}) conditional(s32[]{:T(128)} %convert_element_type.13, () %tuple.62, (s32[]{:T(128)}, f32[4,4,4]{2,0,1:T(4,128)}, s32[4,4,2]{1,2,0:T(2,128)S(1)}, f32[2,2,128,128]{3,2,1,0:T(8,128)S(1)}, f32[4,4,2,128,128]{4,3,2,1,0:T(8,128)S(1)}) %tuple.63), branch_computations={%region_1.1_spmd, %region_2.2_spmd} | conditional | flops 3258974208 | bytes 39848536 | solution.py:57
  1082.9 3.0 fusion.57
  1107.5 3.0 fusion.59
  1119.1 3.7 fusion.60
  1132.6 136.9 %all-reduce.5.cloned.1.call-done = f32[2,128,128]{1,2,0:T(8,128)} async-done(((f32[2,128,128]{1,2,0:T(8,128)}), f32[2,128,128]{1,2,0:T(8,128)}) %all-reduce.5.cloned.1.call-update) | async-done | bytes 131088 | tf_op jit(solution)/shard_map/psum | solution.py:89
  1277.9 130.4 %all-reduce.7.cloned.1.call-done = f32[2,128,128]{1,2,0:T(8,128)} async-done(((f32[2,128,128]{1,2,0:T(8,128)}), f32[2,128,128]{1,2,0:T(8,128)}) %all-reduce.7.cloned.1.call-update) | async-done | bytes 131088 | tf_op jit(solution)/shard_map/psum | solution.py:89
  1416.7 130.4 %all-reduce.9.cloned.1.call-done = f32[2,128,128]{1,2,0:T(8,128)} async-done(((f32[2,128,128]{1,2,0:T(8,128)}), f32[2,128,128]{1,2,0:T(8,128)}) %all-reduce.9.cloned.1.call-update) | async-done | bytes 131088 | tf_op jit(solution)/shard_map/psum | solution.py:89
  1555.5 130.5 %all-reduce.11.cloned.1.call-done = f32[2,128,128]{1,2,0:T(8,128)} async-done(((f32[2,128,128]{1,2,0:T(8,128)}), f32[2,128,128]{1,2,0:T(8,128)}) %all-reduce.11.cloned.1.call-update) | async-done | bytes 131088 | tf_op jit(solution)/shard_map/psum | solution.py:89
  (236 shorter events, 218.9 us)
Async XLA Ops:
  7.2 1123.6 %copy-start = (f32[1,4,2,128,128]{4,3,2,1,0:T(8,128)S(1)}, f32[1,4,2,128,128]{4,3,2,1,0:T(8,128)}, u32[]{:S(2)}) copy-start(f32[1,4,2,128,128]{4,3,2,1,0:T(8,128)} %param.14) | copy-start | bytes 1572868
  7.2 63.2 %all-gather.3.cloned.1.call-start = ((), (), s32[]{:S(2)}) async-start(), calls=%async_computation | async-start | bytes 2162688 | tf_op jit(solution)/shard_map/all_gather | solution.py:31
  8.8 1260.7 %all-reduce.5.cloned.1.call-start = ((), (), s32[]{:S(2)}) async-start(), calls=%async_computation.1 | async-start | bytes 262144 | tf_op jit(solution)/shard_map/psum | solution.py:89
  37.6 36.3 %copy-start.2 = (s32[4,4,2]{1,2,0:T(2,128)S(1)}, s32[4,4,2]{1,2,0:T(2,128)}, u32[]{:S(2)}) copy-start(s32[4,4,2]{1,2,0:T(2,128)} %param.12) | copy-start | bytes 388
  74.0 9.8 collective-permute-start
  88.0 8.8 collective-permute-start
  101.1 7.9 collective-permute-start
  113.2 8.9 collective-permute-start
  126.3 7.4 collective-permute-start
  137.9 8.2 collective-permute-start
  150.4 8.5 collective-permute-start
  163.2 8.5 collective-permute-start
  176.0 8.5 collective-permute-start
  188.7 8.5 collective-permute-start
  201.5 8.5 collective-permute-start
  214.2 9.1 collective-permute-start
  227.6 10.5 collective-permute-start
  242.3 12.3 collective-permute-start
  258.9 11.1 collective-permute-start
  274.2 732.2 %collective-permute-start = (f32[2,2,128,128]{3,2,1,0:T(8,128)}, f32[2,2,128,128]{3,2,1,0:T(8,128)S(1)}, u32[]{:S(2)}, u32[]{:S(2)}) collective-permute-start(f32[2,2,128,128]{3,2,1,0:T(8,128)} %get-tuple-element.379), channel_id=1, source_target_pairs={{0,32},{32,64},{64,96},{96,128},{128,160},{160,192},{192,224},{224... | collective-permute-start | bytes 786440 | tf_op jit(solution)/shard_map/while/body/eval_jaxpr/ppermute | solution.py:16
  1013.4 5.5 copy-start.6
  1026.9 5.5 copy-start.5
  1038.6 5.5 copy-start.4
  1050.3 5.5 copy-start.3
  1061.3 8.5 collective-permute-start
  1076.7 5.5 copy-start.6
  1090.3 5.5 copy-start.5
  1101.9 5.5 copy-start.4
  1113.6 5.5 copy-start.3
  1132.5 275.8 %all-reduce.7.cloned.1.call-start = ((), (), s32[]{:S(2)}) async-start(), calls=%async_computation.2 | async-start | bytes 262144 | tf_op jit(solution)/shard_map/psum | solution.py:89
  1277.8 269.3 %all-reduce.9.cloned.1.call-start = ((), (), s32[]{:S(2)}) async-start(), calls=%async_computation.3 | async-start | bytes 262144 | tf_op jit(solution)/shard_map/psum | solution.py:89
  1416.7 269.3 %all-reduce.11.cloned.1.call-start = ((), (), s32[]{:S(2)}) async-start(), calls=%async_computation.4 | async-start | bytes 262144 | tf_op jit(solution)/shard_map/psum | solution.py:89
  (17 other events, 11.8 us)
Sparse Core Ops, SparseCore 0:
  11.7 58.5 all-gather.2
  1132.6 136.8 all-reduce.4
  1278.0 130.3 all-reduce.6
  1416.8 130.2 all-reduce.8
  1555.6 130.3 all-reduce.10
where the time goes:
time: 1730 us; the launch traced here: 1700 us
  waiting for transfers between devices  1420 us (82%)
  matrix products  84 us (5%)
  other arithmetic  63.6 us (4%)
  local copies, waits for them, and re-layouts  57.6 us (3%)
  blocking collectives  25.4 us (1%)
  between operations  24.2 us (1%)
  starting transfers between devices  22 us (1%)
    ppermute x17, waiting for transfers between devices, from_behind(): lax.ppermute(value, axis, [(source, source + steps) for source in range(l...  855 us
    psum x4, waiting for transfers between devices, body(): lax.psum(jnp.einsum('wsik,wskl->sil', product, right_side, precision=lax....  528 us
  transfers between devices with their start and end apart: 22, of which 22 were waited for; matrix products, arithmetic and copies ran while one was open for 0% of the time, Pallas kernels for 0%

commit v1 on v0

v1 whole, which is shorter than its diff:
```python
import functools

import jax
import jax.numpy as jnp
from jax import lax
from jax.experimental import pallas as pl
from jax.experimental.pallas import tpu as pltpu
from jax.sharding import PartitionSpec as P

ITERS = 4
STEP = 0.5
EPSILON = 1e-06
N = 128
ORB = 4
PHYS = 4
SEC = 2
WORK = 4
MESH = pl.DeviceIdType.MESH
F32, BF16 = jnp.float32, jnp.bfloat16


def split(x):
    high = x.astype(BF16)
    return high, (x - high.astype(F32)).astype(BF16)


def dot(a, b):
    return lax.dot_general(a, b, (((1,), (0,)), ((), ())), preferred_element_type=F32)


def kernel(
    sites,
    terms,
    perm_ref,
    coup_ref,
    left_ref,
    mps_ref,
    right_ref,
    start_ref,
    env_ref,
    state_ref,
    energy_ref,
    mine,
    theirs,
    slab,
    full,
    starts,
    weights_b,
    weights_t,
    enter,
    enter_hl,
    right_hl,
    cur,
    tx,
    rx,
    vec,
    part,
    pieces,
    reduced,
    gathered,
    pair_ss,
    pair_rs,
    orb_ss,
    orb_rs,
    fwd_ss,
    fwd_rs,
    vec_ss,
    vec_rs,
    tx_sem,
    rx_sem,
    red_ss,
    red_rs,
    gat_ss,
    gat_rs,
):
    site = lax.axis_index("site")
    me = lax.axis_index("term")
    chip, core = me // 2, me % 2
    chips = terms // 2
    sibling = chip * 2 + (1 - core)
    last = sites - 1

    barrier = pltpu.get_barrier_semaphore()

    def greet(d, carry):
        pl.semaphore_signal(barrier, inc=1, device_id={"term": lax.rem(me + d, terms)}, device_id_type=MESH)
        return carry

    lax.fori_loop(1, terms, greet, 0)

    @pl.when(site > 0)
    def _():
        pl.semaphore_signal(barrier, inc=1, device_id={"site": site - 1}, device_id_type=MESH)

    @pl.when(site < last)
    def _():
        pl.semaphore_signal(barrier, inc=1, device_id={"site": site + 1}, device_id_type=MESH)

    shard = mps_ref[...]
    mine[0 : ORB * 8] = jnp.concatenate([shard, shard], axis=1)
    own = start_ref[...]
    mine[ORB * 8 : ORB * 8 + SEC] = jnp.concatenate([own, own], axis=1)
    greeted = terms - 1 + jnp.where(site > 0, 1, 0) + jnp.where(site < last, 1, 0)
    pl.semaphore_wait(barrier, greeted)

    pair = pltpu.make_async_remote_copy(
        src_ref=mine, dst_ref=theirs, send_sem=pair_ss, recv_sem=pair_rs,
        device_id={"term": sibling}, device_id_type=MESH,
    )
    pair.start()
    pair.wait()
    half = lax.broadcasted_iota(jnp.int32, (ORB * 8 + SEC, 8, N), 1) // 4
    slab[...] = jnp.where(half == core, mine[...], theirs[...])

    def spread(o, carry):
        source = slab.at[pl.ds(o * 8 + core * 4, 4)]
        pltpu.make_async_copy(source, full.at[o, chip, core], orb_rs.at[o]).start()

        def peer_copy(d, c):
            peer = lax.rem(chip + d, chips) * 2 + core
            pltpu.make_async_remote_copy(
                src_ref=source, dst_ref=full.at[o, chip, core], send_sem=orb_ss.at[o], recv_sem=orb_rs.at[o],
                device_id={"term": peer}, device_id_type=MESH,
            ).start()
            return c

        lax.fori_loop(1, chips, peer_copy, 0)
        return carry

    lax.fori_loop(0, ORB, spread, 0)
    vec_source = slab.at[pl.ds(ORB * 8, SEC)]
    pltpu.make_async_copy(vec_source, starts.at[chip], vec_rs).start()

    def vec_copy(d, c):
        peer = lax.rem(chip + d, chips) * 2 + core
        pltpu.make_async_remote_copy(
            src_ref=vec_source, dst_ref=starts.at[chip], send_sem=vec_ss, recv_sem=vec_rs,
            device_id={"term": peer}, device_id_type=MESH,
        ).start()
        return c

    lax.fori_loop(1, chips, vec_copy, 0)

    def prepare_right(w, carry):
        for s in range(SEC):
            high, low = split(right_ref[w, s])
            right_hl[s, pl.ds(w * N, N), 0:N] = high
            right_hl[s, pl.ds(w * N, N), N : 2 * N] = low
        return carry

    lax.fori_loop(0, WORK, prepare_right, 0)

    def forward(o):
        return pltpu.make_async_remote_copy(
            src_ref=full.at[o, :, core], dst_ref=full.at[o, :, core], send_sem=fwd_ss.at[o], recv_sem=fwd_rs.at[o],
            device_id={"term": sibling}, device_id_type=MESH,
        )

    def prepare(o):
        pltpu.make_async_copy(full.at[o, :, core], full.at[o, :, core], orb_rs.at[o]).wait()
        forward(o).start()
        pltpu.make_async_copy(full.at[o, :, 1 - core], full.at[o, :, 1 - core], fwd_rs.at[o]).wait()
        for p in range(PHYS):
            blocks = [full[o, :, p // 2, (p % 2) * SEC + t].reshape(N, N) for t in range(SEC)]
            columns = slice(p * N, (p + 1) * N)
            for t in range(SEC):
                high, low = split(blocks[t])
                weights_t[o, t, 0, :, columns] = high * BF16(0.5)
                weights_t[o, t, 1, :, columns] = low
            first = perm_ref[(o * PHYS + p) * SEC]
            for s in range(SEC):
                block = jnp.where(first == s, blocks[0], blocks[1]).T.astype(BF16)
                weights_b[o, s, 0:N, columns] = block
                weights_b[o, s, N : 2 * N, columns] = block

    def orbital(w, o):
        moved = []
        for s in range(SEC):
            high, low = split(cur[s])
            moved.append(dot(jnp.concatenate([high, low], axis=1), weights_b[o, s]))
        for t in range(SEC):
            highs, lows = [], []
            for p in range(PHYS):
                columns = slice(p * N, (p + 1) * N)
                source = perm_ref[(o * PHYS + p) * SEC + t]
                weight = coup_ref[(w * ORB + o) * PHYS + p]
                high, low = split(jnp.where(source == 0, moved[0][:, columns], moved[1][:, columns]) * weight)
                highs.append(high)
                lows.append(low)
            high, low = jnp.concatenate(highs, axis=0), jnp.concatenate(lows, axis=0)
            wide = dot(weights_t[o, t, 0], jnp.concatenate([high, low], axis=1))
            y = wide[:, :N] + wide[:, N:] + dot(weights_t[o, t, 1], high)
            cur[t] = y + y.T

    row = lax.broadcasted_iota(jnp.int32, (N, N), 0)
    column = lax.broadcasted_iota(jnp.int32, (N, N), 1)

    def advance(w, first):
        cur[...] = enter[w]

        def one(o, carry):
            if first is not None:
                pl.when(first)(lambda: prepare(o))
            orbital(w, o)
            return carry

        lax.fori_loop(0, ORB, one, 0)
        env_ref[w] = cur[...]

    def chain_copy(w):
        return pltpu.make_async_remote_copy(
            src_ref=tx.at[w], dst_ref=rx.at[w], send_sem=tx_sem.at[w], recv_sem=rx_sem.at[w],
            device_id={"site": lax.rem(site + 1, sites)}, device_id_type=MESH,
        )

    @pl.when(site > 0)
    def _():
        def early(o, carry):
            prepare(o)
            return carry

        lax.fori_loop(0, ORB, early, 0)

    def chain(w, carry):
        @pl.when(site == 0)
        def _():
            enter[w] = left_ref[w]

        @pl.when(site > 0)
        def _():
            chain_copy(w).wait_recv()
            packed = rx[w, 0:N]
            flipped = packed.T
            diagonal = rx[w, N : N + 1]
            enter[w, 0] = jnp.where(row <= column, packed, flipped)
            enter[w, 1] = jnp.where(row > column, packed, jnp.where(row < column, flipped, diagonal))

        @pl.when(site < last)
        def _():
            advance(w, jnp.logical_and(site == 0, w == 0))
            tx[w, 0:N] = jnp.where(row <= column, cur[0], cur[1])
            diagonal = jnp.sum(jnp.where(row == column, cur[1], 0.0), axis=0, keepdims=True)
            tx[w, N : N + 8] = jnp.broadcast_to(diagonal, (8, N))
            chain_copy(w).start()

        for s in range(SEC):
            high, low = split(enter[w, s])
            enter_hl[s, pl.ds(w * N, N), 0:N] = high
            enter_hl[s, pl.ds(w * N, N), N : 2 * N] = low
        return carry

    lax.fori_loop(0, WORK, chain, 0)

    entries = SEC * N * N
    pltpu.make_async_copy(starts, starts, vec_rs).wait()
    u = [starts[:, s].reshape(N, N) for s in range(SEC)]
    scale = jnp.sqrt((jnp.sum(u[0] * u[0]) + jnp.sum(u[1] * u[1])) / entries + EPSILON)
    for s in range(SEC):
        vec[s] = u[s] / scale

    def iteration(it, carry):
        slot = lax.rem(it, 2)
        for s in range(SEC):
            high, low = split(vec[s])
            sides = jnp.concatenate(
                [jnp.concatenate([high, low], axis=1), jnp.concatenate([high, jnp.zeros_like(high)], axis=1)], axis=0
            )
            wide = dot(right_hl[s], sides)
            product = wide[:, :N] + wide[:, N:]
            high, low = split(product)
            high = jnp.concatenate([high[w * N : (w + 1) * N] for w in range(WORK)], axis=1)
            low = jnp.concatenate([low[w * N : (w + 1) * N] for w in range(WORK)], axis=1)
            wide = dot(high, enter_hl[s])
            total = wide[:, :N] + wide[:, N:] + dot(low, enter_hl[s, :, 0:N])
            part[slot, pl.ds(s * (N // 8), N // 8)] = total.reshape(N // 8, 8, N)

        pltpu.make_async_copy(part.at[slot, me], pieces.at[slot, me], red_rs.at[slot]).start()

        def scatter(d, c):
            peer = lax.rem(me + d, terms)
            pltpu.make_async_remote_copy(
                src_ref=part.at[slot, peer], dst_ref=pieces.at[slot, me], send_sem=red_ss.at[slot],
                recv_sem=red_rs.at[slot], device_id={"term": peer}, device_id_type=MESH,
            ).start()
            return c

        lax.fori_loop(1, terms, scatter, 0)

        @pl.when(site == last)
        def _():
            advance(it, None)

        pltpu.make_async_copy(pieces.at[slot], pieces.at[slot], red_rs.at[slot]).wait()
        reduced[slot] = jnp.sum(pieces[slot], axis=0) * (1.0 / (WORK * terms))
        pltpu.make_async_copy(reduced.at[slot], gathered.at[slot, me], gat_rs.at[slot]).start()

        def share(d, c):
            peer = lax.rem(me + d, terms)
            pltpu.make_async_remote_copy(
                src_ref=reduced.at[slot], dst_ref=gathered.at[slot, me], send_sem=gat_ss.at[slot],
                recv_sem=gat_rs.at[slot], device_id={"term": peer}, device_id_type=MESH,
            ).start()
            return c

        lax.fori_loop(1, terms, share, 0)
        pltpu.make_async_copy(gathered.at[slot], gathered.at[slot], gat_rs.at[slot]).wait()
        sent = pieces.at[slot, pl.ds(0, terms - 1)]
        pltpu.make_async_copy(sent, sent, red_ss.at[slot]).wait()
        pltpu.make_async_copy(sent, sent, gat_ss.at[slot]).wait()

        image = gathered[slot].reshape(SEC, N, N)
        old = vec[...]
        rayleigh = jnp.sum(old * image) / jnp.sum(old * old)
        corrected = old - STEP * (image - rayleigh * old)
        vec[...] = corrected / jnp.sqrt(jnp.sum(corrected * corrected) / entries + EPSILON)
        energy_ref[0, 0] = rayleigh
        return carry

    lax.fori_loop(0, ITERS, iteration, 0)
    for s in range(SEC):
        rows = vec[s, pl.ds(pl.multiple_of(chip * 8, 8), 8)]
        state_ref[s] = jnp.where(core == 0, rows[0:4], rows[4:8])

    def spread_done(o, carry):
        part_sent = full.at[o, pl.ds(0, chips - 1), 0]
        pltpu.make_async_copy(part_sent, part_sent, orb_ss.at[o]).wait()
        forward(o).wait_send()
        return carry

    lax.fori_loop(0, ORB, spread_done, 0)
    vec_sent = starts.at[pl.ds(0, chips - 1)]
    pltpu.make_async_copy(vec_sent, vec_sent, vec_ss).wait()

    @pl.when(site < last)
    def _():
        def chain_done(w, carry):
            chain_copy(w).wait_send()
            return carry

        lax.fori_loop(0, WORK, chain_done, 0)


def solution(mesh):
    sites, terms = mesh.shape["site"], mesh.shape["term"]
    chips = terms // 2

    def body(left_edge, mps, block_list, coupling, right_env, start_vector):
        shard = jnp.swapaxes(mps, 3, 4).reshape(ORB * 8, 4, N)
        start = jnp.swapaxes(start_vector[0], 1, 2)
        vmem = pl.BlockSpec(memory_space=pltpu.VMEM)
        smem = pl.BlockSpec(memory_space=pltpu.SMEM)
        dma = pltpu.SemaphoreType.DMA
        env, state, energy = pl.pallas_call(
            functools.partial(kernel, sites, terms),
            out_shape=(
                jax.ShapeDtypeStruct((WORK, SEC, N, N), F32),
                jax.ShapeDtypeStruct((SEC, 4, N), F32),
                jax.ShapeDtypeStruct((1, 1), F32),
            ),
            in_specs=[smem, smem, vmem, vmem, vmem, vmem],
            out_specs=(vmem, vmem, smem),
            scratch_shapes=[
                pltpu.VMEM((ORB * 8 + SEC, 8, N), F32),
                pltpu.VMEM((ORB * 8 + SEC, 8, N), F32),
                pltpu.VMEM((ORB * 8 + SEC, 8, N), F32),
                pltpu.VMEM((ORB, chips, 2, 4, 8, N), F32),
                pltpu.VMEM((chips, SEC, 8, N), F32),
                pltpu.VMEM((ORB, SEC, 2 * N, PHYS * N), BF16),
                pltpu.VMEM((ORB, SEC, 2, N, PHYS * N), BF16),
                pltpu.VMEM((WORK, SEC, N, N), F32),
                pltpu.VMEM((SEC, WORK * N, 2 * N), BF16),
                pltpu.VMEM((SEC, WORK * N, 2 * N), BF16),
                pltpu.VMEM((SEC, N, N), F32),
                pltpu.VMEM((WORK, N + 8, N), F32),
                pltpu.VMEM((WORK, N + 8, N), F32),
                pltpu.VMEM((SEC, N, N), F32),
                pltpu.VMEM((2, terms, 8, N), F32),
                pltpu.VMEM((2, terms, 8, N), F32),
                pltpu.VMEM((2, 8, N), F32),
                pltpu.VMEM((2, terms, 8, N), F32),
                dma, dma, dma((ORB,)), dma((ORB,)), dma((ORB,)), dma((ORB,)), dma, dma,
                dma((WORK,)), dma((WORK,)), dma((2,)), dma((2,)), dma((2,)), dma((2,)),
            ],
            compiler_params=pltpu.CompilerParams(
                collective_id=0, has_side_effects=True, vmem_limit_bytes=40 * 1024 * 1024
            ),
        )(block_list.reshape(-1), coupling.reshape(-1), left_edge, shard, right_env[0], start)
        return env[None], jnp.swapaxes(state, 1, 2)[None], energy.reshape(1)

    in_specs = (
        P("term", None, None, None),
        P("site", None, None, None, "term"),
        P("site", None, None),
        P("term", "site", None),
        P("site", "term", None, None, None),
        P("site", None, None, "term"),
    )
    out_specs = (P("site", "term", None, None, None), P("site", None, None, "term"), P("site"))
    return jax.shard_map(body, mesh=mesh, in_specs=in_specs, out_specs=out_specs, check_vma=False)
```

time: 1730 us -> 172 us (0.10); the launches traced: 1700 us -> 172 us
  waiting for transfers between devices: 1420 us -> 0 us
  Pallas kernels: 0 us -> 164 us
  matrix products: 84 us -> 0 us
  other arithmetic: 63.6 us -> 0 us
  local copies, waits for them, and re-layouts: 57.6 us -> 5.9 us
  blocking collectives: 25.4 us -> 0 us
  starting transfers between devices: 22 us -> 0 us
  between operations: 24.2 us -> 2.35 us
    ppermute x17 -> x0, waiting for transfers between devices: 855 us -> none  [from_behind(): lax.ppermute(value, axis, [(source, source + steps) for source in range(l...]
    psum x4 -> x0, waiting for transfers between devices: 528 us -> none  [body(): lax.psum(jnp.einsum('wsik,wskl->sil', product, right_side, precision=lax....]
    pallas_call x0 -> x1, Pallas kernels: none -> 164 us  [body(): pl.pallas_call(functools.partial(kernel, sites, terms), out_shape=(jax.Sh...]
    dot_general x40 -> x0, matrix products: 84 us -> none  [the longest x8 25.6 us: env_step(): jnp.einsum('wp,wptik->wtik', weights, sandwich, precision=lax.Precision.H...]
    all_gather x1 -> x0, waiting for transfers between devices: 32.7 us -> none  [body(): blocks = lax.all_gather(mps, 'term', axis=4, tiled=True)]
    dynamic_update_slice x17 -> x0, other arithmetic: 28.8 us -> none  [chain_step(): lax.dynamic_update_slice_in_dim(leaving, jnp.where(valid, produced, curre...]
    all_gather x1 -> x0, blocking collectives: 25.4 us -> none  [body(): vector = lax.all_gather(start_vector[0], 'term', axis=2, tiled=True)]
    ppermute x17 -> x0, starting transfers between devices: 21.8 us -> none  [from_behind(): lax.ppermute(value, axis, [(source, source + steps) for source in range(l...]
  transfers between devices with their start and end apart: 22 -> 0, of which waited for: 22 -> 0; matrix products, arithmetic and copies ran while one was open for 0% -> 0% of each run, Pallas kernels for 0% -> 0%
where the time goes in v1:
time: 172 us
  Pallas kernels  164 us (95%)
  local copies, waits for them, and re-layouts  5.9 us (3%)
  between operations  2.35 us (1%)
    pallas_call x1, Pallas kernels, body(): pl.pallas_call(functools.partial(kernel, sites, terms), out_shape=(jax.Sh...  164 us
    unnamed x13, local copies, waits for them, and re-layouts  5.02 us

profile of v1, /device:TPU:481, one launch (start us, length us, event | category | flops | bytes accessed | tf_op | source)
XLA Modules:
  0.0 171.8 jit_solution(3348304002275231798)
XLA Ops:
  0.6 0.0 copy-start.4
  0.6 0.8 reshape.19.coup_ref
  1.4 0.0 copy-done.4
  1.4 0.1 copy.10
  1.6 0.0 copy-start.3
  1.6 0.1 reshape.18.perm_ref
  1.6 0.6 copy-done.3
  2.2 0.0 copy-start
  2.2 1.0 copy-done
  3.3 0.0 copy-start.1
  3.3 1.0 copy-done.1
  4.3 0.0 copy-start.2
  4.3 0.8 copy-done.2
  5.2 163.6 %shard_map.85 = (f32[4,2,128,128]{3,2,1,0:T(8,128)S(1)}, f32[2,4,128]{2,1,0:T(4,128)S(1)}, f32[1,1]{1,0:T(1,128)}) custom-call(s32[32]{0:T(128)S(1)} %reshape.18.perm_ref, f32[64]{0:T(128)S(1)} %reshape.19.coup_ref, f32[4,2,128,128]{3,2,1,0:T(8,128)S(1)} %copy-done, f32[32,4,128]{2,1,0:T(4,128)S(1)} %bitcast.14, f32[4,2,128,128]{3,2,1,0:T(8,128)S(1)} %bitcast.12, ...), custom_call_target="tpu_custom_call" | custom-call | tf_op jit(solution)/shard_map/pallas_call | solution.py:353
  168.8 0.8 copy.14
  169.6 0.6 copy.15
Async XLA Ops:
  0.6 0.8 copy-start.4
  1.6 0.7 copy-start.3
  2.2 1.0 copy-start
  3.3 1.0 copy-start.1
  4.3 0.8 copy-start.2

commit v2 on v1

v2 whole, which is shorter than its diff:
```python
import functools

import jax
import jax.numpy as jnp
from jax import lax
from jax.experimental import pallas as pl
from jax.experimental.pallas import tpu as pltpu
from jax.sharding import PartitionSpec as P

ITERS = 4
STEP = 0.5
EPSILON = 1e-06
N = 128
ORB = 4
PHYS = 4
SEC = 2
WORK = 4
PLANES = 4
GROUPS = ((0, 2, 0, 3), (2, 3, 2, 5), (5, 5, 3, 6), (10, 6, 5, 9))
DEEP = max(group[1] for group in GROUPS)
SIDE = 4
MESH = pl.DeviceIdType.MESH
F32, BF16 = jnp.float32, jnp.bfloat16


def split(x):
    high = x.astype(BF16)
    return high, (x - high.astype(F32)).astype(BF16)


def dot(a, b):
    return lax.dot_general(a, b, (((1,), (0,)), ((), ())), preferred_element_type=F32)


def by_plane(plane, field):
    value = jnp.int32(GROUPS[0][field])
    for index, group in enumerate(GROUPS):
        value = jnp.where(plane >= index * PLANES, group[field], value)
    return value


def first_plane(segment):
    value = jnp.int32(0)
    for index, group in enumerate(GROUPS):
        value = jnp.where(segment >= group[0], index * PLANES, value)
    return value


def greetings(sites):
    carrier = {}
    for index, (first, depth, _, _) in enumerate(GROUPS):
        for segment in range(first, first + depth):
            carrier[segment] = index * PLANES
    early, late = set(), set()
    for segment, base in carrier.items():
        early |= {(segment, base + r) for r in range(PLANES)}
        for r in range(PLANES):
            late.add((base + r, segment))
            if segment + 1 < sites:
                late |= {(base + r, carrier[segment + 1] + r), (base + r, segment + 1)}
    early = {(a, b) for a, b in early if a != b}
    late = {(a, b) for a, b in late if a != b and (a, b) not in early}
    return {(b, a) for a, b in early} | late, {(b, a) for a, b in late}


def lookup(site, values):
    chosen = jnp.int32(0)
    for plane, value in enumerate(values):
        chosen = jnp.where(site == plane, value, chosen)
    return chosen


def kernel(
    sites,
    terms,
    perm_ref,
    coup_ref,
    left_ref,
    mps_ref,
    right_ref,
    start_ref,
    env_ref,
    state_ref,
    energy_ref,
    left_in,
    mps_in,
    right_in,
    start_in,
    mine,
    theirs,
    slab,
    slabs,
    coef,
    lanes,
    coefs,
    full,
    starts,
    weights_b,
    weights_t,
    enter_hl,
    right_hl,
    cur,
    tx,
    rx,
    vec,
    part,
    pieces,
    reduced,
    gathered,
    pair_ss,
    pair_rs,
    slab_ss,
    slab_rs,
    coef_ss,
    coef_rs,
    leg_ss,
    leg_rs,
    orb_ss,
    orb_rs,
    fwd_ss,
    fwd_rs,
    vec_ss,
    vec_rs,
    tx_sem,
    rx_sem,
    red_ss,
    red_rs,
    gat_ss,
    gat_rs,
    load_sem,
    answered,
):
    site = lax.axis_index("site")
    me = lax.axis_index("term")
    chip, core = me // 2, me % 2
    chips = terms // 2
    sibling = chip * 2 + (1 - core)
    last = sites - 1
    first, depth, ready, steps = (by_plane(site, field) for field in range(4))
    term = lax.rem(site, PLANES)
    x, y = chip % SIDE, chip // SIDE

    loads = [
        pltpu.make_async_copy(outside, inside, load_sem.at[index])
        for index, (outside, inside) in enumerate(
            ((mps_ref, mps_in), (start_ref, start_in), (left_ref, left_in), (right_ref, right_in))
        )
    ]
    for load in loads:
        load.start()

    def along_x(d):
        return {"term": (y * SIDE + lax.rem(x + d, SIDE)) * 2 + core}

    def along_y(d):
        return {"term": (lax.rem(y + d, SIDE) * SIDE + x) * 2 + core}

    barrier = pltpu.get_barrier_semaphore()
    for d in range(1, SIDE):
        for line in (along_x, along_y):
            pl.semaphore_signal(barrier, inc=1, device_id=line(d), device_id_type=MESH)
    pl.semaphore_signal(barrier, inc=1, device_id={"term": sibling}, device_id_type=MESH)
    entry, answers = greetings(sites)

    def signal_planes(pairs, semaphore):
        mask = lookup(site, [sum(1 << b for a, b in pairs if a == plane) for plane in range(sites)])

        def one(other, carry):
            @pl.when((mask >> other) % 2 == 1)
            def _():
                pl.semaphore_signal(semaphore, inc=1, device_id={"site": other}, device_id_type=MESH)

            return carry

        lax.fori_loop(0, sites, one, 0)

    def greeted(pairs):
        return lookup(site, [sum(1 for a, b in pairs if b == plane) for plane in range(sites)])

    signal_planes(entry, barrier)

    loads[0].wait()
    loads[1].wait()
    shard = mps_in[...]
    shard = jnp.concatenate([shard, shard], axis=1).reshape(ORB, 2, 4, 8, N)
    for h in range(2):
        mine[h * 16 : (h + 1) * 16] = shard[:, h].reshape(16, 8, N)
    own = start_in[...]
    mine[32 : 32 + SEC] = jnp.concatenate([own, own], axis=1)

    lane = lax.broadcasted_iota(jnp.int32, (8, N), 1)

    compact = jnp.zeros((8, N), F32)
    for w in range(WORK):
        for o in range(ORB):
            for p in range(PHYS):
                compact = jnp.where(lane == (w * ORB + o) * PHYS + p, coup_ref[w, o, p], compact)
    for o in range(ORB):
        for p in range(PHYS):
            for t in range(SEC):
                index = WORK * ORB * PHYS + (o * PHYS + p) * SEC + t
                compact = jnp.where(lane == index, perm_ref[o, p, t].astype(F32), compact)
    coef[...] = compact
    pl.semaphore_wait(barrier, 2 * (SIDE - 1) + 1 + greeted(entry))
    signal_planes(answers, answered)

    pair = pltpu.make_async_remote_copy(
        src_ref=mine, dst_ref=theirs, send_sem=pair_ss, recv_sem=pair_rs,
        device_id={"term": sibling}, device_id_type=MESH,
    )
    pair.start()
    pair.wait()
    half = lax.broadcasted_iota(jnp.int32, (32 + SEC, 8, N), 1) // 4
    slab[...] = jnp.where(half == core, mine[...], theirs[...])

    source = slab.at[pl.ds(core * 16, 16)]
    to_base = first_plane(site)

    place_of = site - by_plane(to_base, 0)

    def slab_copies(r):
        return [
            pltpu.make_async_remote_copy(
                src_ref=src, dst_ref=dst, send_sem=ss.at[r], recv_sem=rs.at[place_of],
                device_id={"site": to_base + r}, device_id_type=MESH,
            )
            for src, dst, ss, rs in (
                (source, slabs.at[place_of], slab_ss, slab_rs),
                (coef, lanes.at[place_of], coef_ss, coef_rs),
            )
        ]

    def slab_send(r, carry):
        @pl.when(to_base + r == site)
        def _():
            pltpu.make_async_copy(source, slabs.at[place_of], slab_rs.at[place_of]).start()
            pltpu.make_async_copy(coef, lanes.at[place_of], coef_rs.at[place_of]).start()

        @pl.when(to_base + r != site)
        def _():
            for copy in slab_copies(r):
                copy.start()

        return carry

    lax.fori_loop(0, PLANES, slab_send, 0)

    def tiles_of(o):
        return pl.ds(o * 4, 4)

    def row_of(q, o, r):
        return full.at[q, r, :, core, tiles_of(o)]

    def column_of(q, o, c):
        return full.at[q, :, c, core, tiles_of(o)]

    def first_leg(q, o):
        place = full.at[q, y, x, core, tiles_of(o)]
        tiles = slabs.at[q, tiles_of(o)]
        pltpu.make_async_copy(tiles, place, leg_rs.at[q, o]).start()
        for d in range(1, SIDE):
            pltpu.make_async_remote_copy(
                src_ref=tiles, dst_ref=place, send_sem=leg_ss.at[q], recv_sem=leg_rs.at[q, o],
                device_id=(along_x, along_y)[o % 2](d), device_id_type=MESH,
            ).start()

    def second_leg(q, o):
        line = row_of(q, o, y) if o % 2 == 0 else column_of(q, o, x)
        pltpu.make_async_copy(line, line, leg_rs.at[q, o]).wait()
        for d in range(1, SIDE):
            pltpu.make_async_remote_copy(
                src_ref=line, dst_ref=line, send_sem=orb_ss.at[q], recv_sem=orb_rs.at[q, o, d - 1],
                device_id=(along_y, along_x)[o % 2](d), device_id_type=MESH,
            ).start()

    def arrived(q, o, parity):
        for d in range(1, SIDE):
            if parity == 0:
                line = row_of(q, o, lax.rem(y + SIDE - d, SIDE))
            else:
                line = column_of(q, o, lax.rem(x + SIDE - d, SIDE))
            pltpu.make_async_copy(line, line, orb_rs.at[q, o, d - 1]).wait()

    def forward(q, o):
        tiles = full.at[q, :, :, core, tiles_of(o)]
        return pltpu.make_async_remote_copy(
            src_ref=tiles, dst_ref=tiles, send_sem=fwd_ss.at[q, o], recv_sem=fwd_rs.at[q, o],
            device_id={"term": sibling}, device_id_type=MESH,
        )

    def gather_step(i):
        @pl.when(i < depth)
        def _():
            pltpu.make_async_copy(slabs.at[i], slabs.at[i], slab_rs.at[i]).wait()
            pltpu.make_async_copy(lanes.at[i], lanes.at[i], coef_rs.at[i]).wait()
            for o in range(ORB):
                first_leg(i, o)
            coefs[i] = jnp.broadcast_to(lanes[i, 0:1], (N, N)).T

        @pl.when(jnp.logical_and(i >= 1, i < depth + 1))
        def _():
            for o in range(ORB):
                second_leg(i - 1, o)

        @pl.when(jnp.logical_and(i >= 3, i < depth + 3))
        def _():
            for o in range(ORB):
                arrived(i - 3, o, o % 2)
                forward(i - 3, o).start()

    def gather_loop(i, carry):
        gather_step(i)
        return carry

    lax.fori_loop(0, steps, gather_loop, 0)

    vec_source = slab.at[pl.ds(32, SEC)]

    def side_work():
        pltpu.make_async_copy(vec_source, starts.at[chip], vec_rs).start()

        def vec_copy(d, c):
            peer = lax.rem(chip + d, chips) * 2 + core
            pltpu.make_async_remote_copy(
                src_ref=vec_source, dst_ref=starts.at[chip], send_sem=vec_ss, recv_sem=vec_rs,
                device_id={"term": peer}, device_id_type=MESH,
            ).start()
            return c

        lax.fori_loop(1, chips, vec_copy, 0)

        loads[3].wait()

        def prepare_right(w, carry):
            for s in range(SEC):
                high, low = split(right_in[w, s])
                right_hl[s, pl.ds(w * N, N), 0:N] = high
                right_hl[s, pl.ds(w * N, N), N : 2 * N] = low
            return carry

        lax.fori_loop(0, WORK, prepare_right, 0)

    pl.when(ready > 0)(side_work)

    def coefficient(q, index):
        return coefs[q, pl.ds(index, 1)]

    def sector(q, o, p, t):
        return coefficient(q, WORK * ORB * PHYS + (o * PHYS + p) * SEC + t)

    def prepare(q, o):
        there = full.at[q, :, :, 1 - core, tiles_of(o)]
        pltpu.make_async_copy(there, there, fwd_rs.at[q, o]).wait()
        for p in range(PHYS):
            blocks = [full[q, :, :, p // 2, o * 4 + (p % 2) * SEC + t].reshape(N, N) for t in range(SEC)]
            columns = slice(p * N, (p + 1) * N)
            for t in range(SEC):
                high, low = split(blocks[t])
                weights_t[q, o, t, 0, :, columns] = high * BF16(0.5)
                weights_t[q, o, t, 1, :, columns] = low
            source_of_first = sector(q, o, p, 0)
            for s in range(SEC):
                weights_b[q, o, s, :, columns] = jnp.where(source_of_first == s, blocks[0], blocks[1]).T.astype(BF16)

    def orbital(q, o):
        moved = []
        for s in range(SEC):
            high, low = split(cur[s])
            block = weights_b[q, o, s]
            moved.append(dot(jnp.concatenate([high, low], axis=1), jnp.concatenate([block, block], axis=0)))
        for t in range(SEC):
            highs, lows = [], []
            for p in range(PHYS):
                columns = slice(p * N, (p + 1) * N)
                source_sector = sector(q, o, p, t)
                weight = coefficient(q, (term * ORB + o) * PHYS + p)
                high, low = split(jnp.where(source_sector == 0, moved[0][:, columns], moved[1][:, columns]) * weight)
                highs.append(high)
                lows.append(low)
            high, low = jnp.concatenate(highs, axis=0), jnp.concatenate(lows, axis=0)
            wide = dot(weights_t[q, o, t, 0], jnp.concatenate([high, low], axis=1))
            y = wide[:, :N] + wide[:, N:] + dot(weights_t[q, o, t, 1], high)
            cur[t] = y + y.T

    row = lax.broadcasted_iota(jnp.int32, (N, N), 0)
    column = lax.broadcasted_iota(jnp.int32, (N, N), 1)

    def unpack(kind, w):
        packed = rx[kind, w, 0:N]
        flipped = packed.T
        diagonal = rx[kind, w, N : N + 1]
        return (
            jnp.where(row <= column, packed, flipped),
            jnp.where(row > column, packed, jnp.where(row < column, flipped, diagonal)),
        )

    def message(kind, w, slot, plane):
        return pltpu.make_async_remote_copy(
            src_ref=tx.at[slot], dst_ref=rx.at[kind, w], send_sem=tx_sem.at[kind, slot], recv_sem=rx_sem.at[kind, w],
            device_id={"site": plane}, device_id_type=MESH,
        )

    def received(kind, w):
        pltpu.make_async_copy(rx.at[kind, w], rx.at[kind, w], rx_sem.at[kind, w]).wait()

    def act(copy, start):
        if start:
            copy.start()
        else:
            copy.wait_send()

    def messages(q, start):
        segment = first + q
        after = lax.rem(segment + 1, sites)
        goes_on = jnp.logical_and(q == depth - 1, segment < last)
        pl.when(goes_on)(lambda: act(message(0, term, q, first_plane(after) + term), start))
        pl.when(jnp.logical_and(segment < last, after != site))(lambda: act(message(1, term, q, after), start))
        if start:

            @pl.when(jnp.logical_and(segment < last, after == site))
            def _():
                pltpu.make_async_copy(tx.at[q], rx.at[1, term], rx_sem.at[1, term]).start()

    def results(q, start):
        pl.when(first + q != site)(lambda: act(message(2, term, q, first + q), start))

    def early(index, carry):
        prepare(index // ORB, index % ORB)
        return carry

    lax.fori_loop(0, ready * ORB, early, 0)
    loads[2].wait()
    pl.semaphore_wait(answered, greeted(answers))

    @pl.when(first == 0)
    def _():
        cur[...] = left_in[term]

    @pl.when(first > 0)
    def _():
        received(0, term)
        cur[0], cur[1] = unpack(0, term)

    def one_segment(q, c):
        pl.when(q + 3 >= steps)(lambda: gather_step(q + 3))

        def one(o, cc):
            pl.when(q >= ready)(lambda: prepare(q, o))
            orbital(q, o)
            return cc

        lax.fori_loop(0, ORB, one, 0)
        tx[q, 0:N] = jnp.where(row <= column, cur[0], cur[1])
        diagonal = jnp.sum(jnp.where(row == column, cur[1], 0.0), axis=0, keepdims=True)
        tx[q, N : N + 8] = jnp.broadcast_to(diagonal, (8, N))
        messages(q, True)

        @pl.when(first + q == site)
        def _():
            env_ref[term] = cur[...]

        return c

    lax.fori_loop(0, depth, one_segment, 0)

    def results_start(q, carry):
        results(q, True)
        return carry

    lax.fori_loop(0, depth, results_start, 0)
    pl.when(ready == 0)(side_work)

    def entering(w, carry):
        pl.when(site > 0)(lambda: received(1, w))

        def keep(blocks):
            for s in range(SEC):
                high, low = split(blocks[s])
                enter_hl[s, pl.ds(w * N, N), 0:N] = high
                enter_hl[s, pl.ds(w * N, N), N : 2 * N] = low

        pl.when(site == 0)(lambda: keep((left_in[w, 0], left_in[w, 1])))
        pl.when(site > 0)(lambda: keep(unpack(1, w)))
        return carry

    lax.fori_loop(0, WORK, entering, 0)

    entries = SEC * N * N
    pltpu.make_async_copy(starts, starts, vec_rs).wait()
    u = [starts[:, s].reshape(N, N) for s in range(SEC)]
    scale = jnp.sqrt((jnp.sum(u[0] * u[0]) + jnp.sum(u[1] * u[1])) / entries + EPSILON)
    for s in range(SEC):
        vec[s] = u[s] / scale

    def total_of(values):
        return jnp.sum(values, axis=(0, 1, 2), keepdims=True)

    offsets = sorted(
        ((a, b, c) for a in range(SIDE) for b in range(SIDE) for c in range(2) if (a, b, c) != (0, 0, 0)),
        key=lambda abc: -min(abc[0], SIDE - abc[0]) - min(abc[1], SIDE - abc[1]),
    )
    far_first = [
        (lax.rem(y + a, SIDE) * SIDE + lax.rem(x + b, SIDE)) * 2 + (core if c == 0 else 1 - core) for a, b, c in offsets
    ]

    def iteration(it, carry):
        slot = lax.rem(it, 2)
        for s in range(SEC):
            high, low = split(vec[s])
            sides = jnp.concatenate(
                [jnp.concatenate([high, low], axis=1), jnp.concatenate([high, jnp.zeros_like(high)], axis=1)], axis=0
            )
            wide = dot(right_hl[s], sides)
            product = wide[:, :N] + wide[:, N:]
            high, low = split(product)
            high = jnp.concatenate([high[w * N : (w + 1) * N] for w in range(WORK)], axis=1)
            low = jnp.concatenate([low[w * N : (w + 1) * N] for w in range(WORK)], axis=1)
            wide = dot(high, enter_hl[s])
            total = wide[:, :N] + wide[:, N:] + dot(low, enter_hl[s, :, 0:N])
            part[slot, pl.ds(s * (N // 8), N // 8)] = total.reshape(N // 8, 8, N)

        pltpu.make_async_copy(part.at[slot, me], pieces.at[slot, me], red_rs.at[slot]).start()

        for peer in far_first:
            pltpu.make_async_remote_copy(
                src_ref=part.at[slot, peer], dst_ref=pieces.at[slot, me], send_sem=red_ss.at[slot],
                recv_sem=red_rs.at[slot], device_id={"term": peer}, device_id_type=MESH,
            ).start()

        old = vec[...]
        square = total_of(old * old)

        pltpu.make_async_copy(pieces.at[slot], pieces.at[slot], red_rs.at[slot]).wait()
        reduced[slot] = jnp.sum(pieces[slot], axis=0) * (1.0 / (WORK * terms))
        pltpu.make_async_copy(reduced.at[slot], gathered.at[slot, me], gat_rs.at[slot]).start()

        for peer in far_first:
            pltpu.make_async_remote_copy(
                src_ref=reduced.at[slot], dst_ref=gathered.at[slot, me], send_sem=gat_ss.at[slot],
                recv_sem=gat_rs.at[slot], device_id={"term": peer}, device_id_type=MESH,
            ).start()

        pltpu.make_async_copy(gathered.at[slot], gathered.at[slot], gat_rs.at[slot]).wait()
        sent = pieces.at[slot, pl.ds(0, terms - 1)]
        pltpu.make_async_copy(sent, sent, red_ss.at[slot]).wait()
        pltpu.make_async_copy(sent, sent, gat_ss.at[slot]).wait()

        image = gathered[slot].reshape(SEC, N, N)
        rayleigh = total_of(old * image) / square
        corrected = old - STEP * (image - rayleigh * old)
        vec[...] = corrected / jnp.sqrt(total_of(corrected * corrected) / entries + EPSILON)
        energy_ref[...] = jnp.broadcast_to(rayleigh[0], (8, N))
        return carry

    lax.fori_loop(0, ITERS, iteration, 0)
    for s in range(SEC):
        rows = vec[s, pl.ds(pl.multiple_of(chip * 8, 8), 8)]
        state_ref[s] = jnp.where(core == 0, rows[0:4], rows[4:8])

    def leaving(w, carry):
        @pl.when(first_plane(site) + w != site)
        def _():
            received(2, w)
            env_ref[w, 0], env_ref[w, 1] = unpack(2, w)

        return carry

    lax.fori_loop(0, WORK, leaving, 0)

    def slab_done(r, carry):
        @pl.when(to_base + r != site)
        def _():
            for copy in slab_copies(r):
                copy.wait_send()

        return carry

    lax.fori_loop(0, PLANES, slab_done, 0)

    def spread_done(q, carry):
        sent = full.at[q, 0, pl.ds(0, SIDE - 1), 0]
        pltpu.make_async_copy(sent, sent, leg_ss.at[q]).wait()
        sent = full.at[q, pl.ds(0, SIDE - 1), :, 0]
        pltpu.make_async_copy(sent, sent, orb_ss.at[q]).wait()
        for o in range(ORB):
            forward(q, o).wait_send()
        return carry

    lax.fori_loop(0, depth, spread_done, 0)
    vec_sent = starts.at[pl.ds(0, chips - 1)]
    pltpu.make_async_copy(vec_sent, vec_sent, vec_ss).wait()

    def messages_done(q, carry):
        messages(q, False)
        results(q, False)
        return carry

    lax.fori_loop(0, depth, messages_done, 0)


def solution(mesh):
    sites, terms = mesh.shape["site"], mesh.shape["term"]
    chips = terms // 2

    def body(left_edge, mps, block_list, coupling, right_env, start_vector):
        shard = jnp.swapaxes(mps, 3, 4).reshape(ORB * 8, 4, N)
        start = jnp.swapaxes(start_vector[0], 1, 2)
        vmem = pl.BlockSpec(memory_space=pltpu.VMEM)
        anywhere = pl.BlockSpec(memory_space=pl.ANY)
        smem = pl.BlockSpec(memory_space=pltpu.SMEM)
        dma = pltpu.SemaphoreType.DMA
        env, state, energy = pl.pallas_call(
            functools.partial(kernel, sites, terms),
            out_shape=(
                jax.ShapeDtypeStruct((WORK, SEC, N, N), F32),
                jax.ShapeDtypeStruct((SEC, 4, N), F32),
                jax.ShapeDtypeStruct((8, N), F32),
            ),
            in_specs=[smem, smem, anywhere, anywhere, anywhere, anywhere],
            out_specs=(vmem, vmem, vmem),
            scratch_shapes=[
                pltpu.VMEM((WORK, SEC, N, N), F32),
                pltpu.VMEM((ORB * 8, 4, N), F32),
                pltpu.VMEM((WORK, SEC, N, N), F32),
                pltpu.VMEM((SEC, 4, N), F32),
                pltpu.VMEM((32 + SEC, 8, N), F32),
                pltpu.VMEM((32 + SEC, 8, N), F32),
                pltpu.VMEM((32 + SEC, 8, N), F32),
                pltpu.VMEM((DEEP, 16, 8, N), F32),
                pltpu.VMEM((8, N), F32),
                pltpu.VMEM((DEEP, 8, N), F32),
                pltpu.VMEM((DEEP, N, N), F32),
                pltpu.VMEM((DEEP, SIDE, SIDE, 2, 16, 8, N), F32),
                pltpu.VMEM((chips, SEC, 8, N), F32),
                pltpu.VMEM((DEEP, ORB, SEC, N, PHYS * N), BF16),
                pltpu.VMEM((DEEP, ORB, SEC, 2, N, PHYS * N), BF16),
                pltpu.VMEM((SEC, WORK * N, 2 * N), BF16),
                pltpu.VMEM((SEC, WORK * N, 2 * N), BF16),
                pltpu.VMEM((SEC, N, N), F32),
                pltpu.VMEM((DEEP, N + 8, N), F32),
                pltpu.VMEM((3, WORK, N + 8, N), F32),
                pltpu.VMEM((SEC, N, N), F32),
                pltpu.VMEM((2, terms, 8, N), F32),
                pltpu.VMEM((2, terms, 8, N), F32),
                pltpu.VMEM((2, 8, N), F32),
                pltpu.VMEM((2, terms, 8, N), F32),
                dma, dma, dma((PLANES,)), dma((DEEP,)), dma((PLANES,)), dma((DEEP,)),
                dma((DEEP,)), dma((DEEP, ORB)), dma((DEEP,)), dma((DEEP, ORB, SIDE - 1)), dma((DEEP, ORB)), dma((DEEP, ORB)),
                dma, dma, dma((3, DEEP)), dma((3, WORK)), dma((2,)), dma((2,)), dma((2,)), dma((2,)),
                dma((4,)), pltpu.SemaphoreType.REGULAR,
            ],
            compiler_params=pltpu.CompilerParams(
                collective_id=0, has_side_effects=True, vmem_limit_bytes=48 * 1024 * 1024
            ),
        )(block_list, coupling, left_edge, shard, right_env[0], start)
        return env[None], jnp.swapaxes(state, 1, 2)[None], energy[0, 0:1]

    in_specs = (
        P("term", None, None, None),
        P("site", None, None, None, "term"),
        P("site", None, None),
        P("term", "site", None),
        P("site", "term", None, None, None),
        P("site", None, None, "term"),
    )
    out_specs = (P("site", "term", None, None, None), P("site", None, None, "term"), P("site"))
    return jax.shard_map(body, mesh=mesh, in_specs=in_specs, out_specs=out_specs, check_vma=False)
```

time: 172 us -> 151 us (0.88)
  Pallas kernels: 164 us -> 144 us
    pallas_call x1, Pallas kernels: 164 us -> 144 us  [body(): pl.pallas_call(functools.partial(kernel, sites, terms), out_shape=(jax.Sh...]
    unnamed x13 -> x15, local copies, waits for them, and re-layouts: 5.02 us -> 5.66 us
where the time goes in v2:
time: 151 us
  Pallas kernels  144 us (95%)
  local copies, waits for them, and re-layouts  6.18 us (4%)
    pallas_call x1, Pallas kernels, body(): pl.pallas_call(functools.partial(kernel, sites, terms), out_shape=(jax.Sh...  144 us
    unnamed x15, local copies, waits for them, and re-layouts  5.66 us

profile of v2, /device:TPU:481, one launch (start us, length us, event | category | flops | bytes accessed | tf_op | source)
XLA Modules:
  0.0 151.1 jit_solution(4116260598448097430)
XLA Ops:
  0.6 0.0 copy-start.5
  0.6 0.0 copy-start.3
  0.7 0.7 copy-done.5
  1.3 0.0 copy-start.4
  1.3 0.1 copy.9.perm_ref
  1.4 0.0 copy-done.3
  1.4 0.6 copy-done.4
  2.0 0.0 copy-start
  2.0 1.0 copy-done
  3.0 0.0 copy-start.1
  3.1 1.0 copy-done.1
  4.1 0.0 copy-start.2
  4.1 0.8 copy-done.2
  4.9 144.3 %shard_map.85 = (f32[4,2,128,128]{3,2,1,0:T(8,128)S(1)}, f32[2,4,128]{2,1,0:T(4,128)S(1)}, f32[8,128]{1,0:T(8,128)S(1)}) custom-call(s32[4,4,2]{2,1,0:T(4,128)S(1)} %copy.9.perm_ref, f32[4,4,4]{2,1,0:T(4,128)S(1)} %copy-done.3, f32[4,2,128,128]{3,2,1,0:T(8,128)S(1)} %copy-done, f32[32,4,128]{2,1,0:T(4,128)S(1)} %bitcast.14, f32[4,2,128,128]{3,2,1,0:T(8,128)S(1)} %bitcast.12, ...), custom_call_target="tpu_custom_call" | custom-call | tf_op jit(solution)/shard_map/pallas_call | solution.py:612
  149.2 0.5 slice.3
  149.7 0.8 copy.12
  150.5 0.6 copy.13
Async XLA Ops:
  0.6 0.7 copy-start.5
  0.6 0.8 copy-start.3
  1.3 0.7 copy-start.4
  2.0 1.0 copy-start
  3.0 1.0 copy-start.1
  4.1 0.8 copy-start.2

commit v3 on v2

--- a/solution.py
+++ b/solution.py
@@ -16,7 +16,7 @@
 SEC = 2
 WORK = 4
 PLANES = 4
-GROUPS = ((0, 2, 0, 3), (2, 3, 2, 5), (5, 5, 3, 6), (10, 6, 5, 9))
+GROUPS = ((0, 3, 0, 4), (3, 3, 3, 6), (6, 4, 4, 7), (10, 6, 6, 9))
 DEEP = max(group[1] for group in GROUPS)
 SIDE = 4
 MESH = pl.DeviceIdType.MESH
@@ -107,6 +107,7 @@
     pieces,
     reduced,
     gathered,
+    quotient,
     pair_ss,
     pair_rs,
     slab_ss,
@@ -288,25 +289,33 @@
             device_id={"term": sibling}, device_id_type=MESH,
         )
 
+    row = lax.broadcasted_iota(jnp.int32, (N, N), 0)
+    column = lax.broadcasted_iota(jnp.int32, (N, N), 1)
+
+    def turn(i):
+        return lax.rem(i + (site - term - first), depth)
+
     def gather_step(i):
         @pl.when(i < depth)
         def _():
-            pltpu.make_async_copy(slabs.at[i], slabs.at[i], slab_rs.at[i]).wait()
-            pltpu.make_async_copy(lanes.at[i], lanes.at[i], coef_rs.at[i]).wait()
+            q = turn(i)
+            pltpu.make_async_copy(slabs.at[q], slabs.at[q], slab_rs.at[q]).wait()
+            pltpu.make_async_copy(lanes.at[q], lanes.at[q], coef_rs.at[q]).wait()
             for o in range(ORB):
-                first_leg(i, o)
-            coefs[i] = jnp.broadcast_to(lanes[i, 0:1], (N, N)).T
+                first_leg(q, o)
+            rows = jnp.broadcast_to(lanes[q, 0:1], (N, N)).T
+            coefs[q] = jnp.where(row < WORK * ORB * PHYS, jnp.sqrt(rows), rows)
 
         @pl.when(jnp.logical_and(i >= 1, i < depth + 1))
         def _():
             for o in range(ORB):
-                second_leg(i - 1, o)
+                second_leg(turn(i - 1), o)
 
         @pl.when(jnp.logical_and(i >= 3, i < depth + 3))
         def _():
             for o in range(ORB):
-                arrived(i - 3, o, o % 2)
-                forward(i - 3, o).start()
+                arrived(turn(i - 3), o, o % 2)
+                forward(turn(i - 3), o).start()
 
     def gather_loop(i, carry):
         gather_step(i)
@@ -352,7 +361,8 @@
         there = full.at[q, :, :, 1 - core, tiles_of(o)]
         pltpu.make_async_copy(there, there, fwd_rs.at[q, o]).wait()
         for p in range(PHYS):
-            blocks = [full[q, :, :, p // 2, o * 4 + (p % 2) * SEC + t].reshape(N, N) for t in range(SEC)]
+            root = coefficient(q, (term * ORB + o) * PHYS + p)
+            blocks = [full[q, :, :, p // 2, o * 4 + (p % 2) * SEC + t].reshape(N, N) * root for t in range(SEC)]
             columns = slice(p * N, (p + 1) * N)
             for t in range(SEC):
                 high, low = split(blocks[t])
@@ -363,27 +373,28 @@
                 weights_b[q, o, s, :, columns] = jnp.where(source_of_first == s, blocks[0], blocks[1]).T.astype(BF16)
 
     def orbital(q, o):
+        sides = [jnp.concatenate(split(cur[s]), axis=1) for s in range(SEC)]
+        pairs = [slice(g * 2 * N, (g + 1) * 2 * N) for g in range(PHYS // 2)]
         moved = []
-        for s in range(SEC):
-            high, low = split(cur[s])
-            block = weights_b[q, o, s]
-            moved.append(dot(jnp.concatenate([high, low], axis=1), jnp.concatenate([block, block], axis=0)))
+        for pair_columns in pairs:
+            blocks = [weights_b[q, o, s, :, pair_columns] for s in range(SEC)]
+            moved.append([dot(sides[s], jnp.concatenate([blocks[s], blocks[s]], axis=0)) for s in range(SEC)])
+        totals = [None] * SEC
+        for g, pair_columns in enumerate(pairs):
+            for t in range(SEC):
+                highs, lows = [], []
+                for within in range(2):
+                    columns = slice(within * N, (within + 1) * N)
+                    chosen = sector(q, o, g * 2 + within, t) == 0
+                    high, low = split(jnp.where(chosen, moved[g][0][:, columns], moved[g][1][:, columns]))
+                    highs.append(high)
+                    lows.append(low)
+                high, low = jnp.concatenate(highs, axis=0), jnp.concatenate(lows, axis=0)
+                wide = dot(weights_t[q, o, t, 0, :, pair_columns], jnp.concatenate([high, low], axis=1))
+                y = wide[:, :N] + wide[:, N:] + dot(weights_t[q, o, t, 1, :, pair_columns], high)
+                totals[t] = y if g == 0 else totals[t] + y
         for t in range(SEC):
-            highs, lows = [], []
-            for p in range(PHYS):
-                columns = slice(p * N, (p + 1) * N)
-                source_sector = sector(q, o, p, t)
-                weight = coefficient(q, (term * ORB + o) * PHYS + p)
-                high, low = split(jnp.where(source_sector == 0, moved[0][:, columns], moved[1][:, columns]) * weight)
-                highs.append(high)
-                lows.append(low)
-            high, low = jnp.concatenate(highs, axis=0), jnp.concatenate(lows, axis=0)
-            wide = dot(weights_t[q, o, t, 0], jnp.concatenate([high, low], axis=1))
-            y = wide[:, :N] + wide[:, N:] + dot(weights_t[q, o, t, 1], high)
-            cur[t] = y + y.T
-
-    row = lax.broadcasted_iota(jnp.int32, (N, N), 0)
-    column = lax.broadcasted_iota(jnp.int32, (N, N), 1)
+            cur[t] = totals[t] + totals[t].T
 
     def unpack(kind, w):
         packed = rx[kind, w, 0:N]
@@ -425,7 +436,7 @@
         pl.when(first + q != site)(lambda: act(message(2, term, q, first + q), start))
 
     def early(index, carry):
-        prepare(index // ORB, index % ORB)
+        prepare(turn(index // ORB), index % ORB)
         return carry
 
     lax.fori_loop(0, ready * ORB, early, 0)
@@ -444,12 +455,13 @@
     def one_segment(q, c):
         pl.when(q + 3 >= steps)(lambda: gather_step(q + 3))
 
-        def one(o, cc):
-            pl.when(q >= ready)(lambda: prepare(q, o))
+        def inline(o, cc):
+            prepare(q, o)
+            return cc
+
+        lax.fori_loop(0, jnp.where(q >= ready, ORB, 0), inline, 0)
+        for o in range(ORB):
             orbital(q, o)
-            return cc
-
-        lax.fori_loop(0, ORB, one, 0)
         tx[q, 0:N] = jnp.where(row <= column, cur[0], cur[1])
         diagonal = jnp.sum(jnp.where(row == column, cur[1], 0.0), axis=0, keepdims=True)
         tx[q, N : N + 8] = jnp.broadcast_to(diagonal, (8, N))
@@ -549,10 +561,11 @@
         rayleigh = total_of(old * image) / square
         corrected = old - STEP * (image - rayleigh * old)
         vec[...] = corrected / jnp.sqrt(total_of(corrected * corrected) / entries + EPSILON)
-        energy_ref[...] = jnp.broadcast_to(rayleigh[0], (8, N))
+        quotient[...] = jnp.broadcast_to(rayleigh[0], (8, N))
         return carry
 
     lax.fori_loop(0, ITERS, iteration, 0)
+    energy_ref[0, 0] = quotient[0, 0]
     for s in range(SEC):
         rows = vec[s, pl.ds(pl.multiple_of(chip * 8, 8), 8)]
         state_ref[s] = jnp.where(core == 0, rows[0:4], rows[4:8])
@@ -606,7 +619,7 @@
         shard = jnp.swapaxes(mps, 3, 4).reshape(ORB * 8, 4, N)
         start = jnp.swapaxes(start_vector[0], 1, 2)
         vmem = pl.BlockSpec(memory_space=pltpu.VMEM)
-        anywhere = pl.BlockSpec(memory_space=pl.ANY)
+        anywhere = pl.BlockSpec(memory_space=pltpu.HBM)
         smem = pl.BlockSpec(memory_space=pltpu.SMEM)
         dma = pltpu.SemaphoreType.DMA
         env, state, energy = pl.pallas_call(
@@ -614,10 +627,10 @@
             out_shape=(
                 jax.ShapeDtypeStruct((WORK, SEC, N, N), F32),
                 jax.ShapeDtypeStruct((SEC, 4, N), F32),
-                jax.ShapeDtypeStruct((8, N), F32),
+                jax.ShapeDtypeStruct((1, 1), F32),
             ),
             in_specs=[smem, smem, anywhere, anywhere, anywhere, anywhere],
-            out_specs=(vmem, vmem, vmem),
+            out_specs=(vmem, vmem, smem),
             scratch_shapes=[
                 pltpu.VMEM((WORK, SEC, N, N), F32),
                 pltpu.VMEM((ORB * 8, 4, N), F32),
@@ -644,16 +657,17 @@
                 pltpu.VMEM((2, terms, 8, N), F32),
                 pltpu.VMEM((2, 8, N), F32),
                 pltpu.VMEM((2, terms, 8, N), F32),
+                pltpu.VMEM((8, N), F32),
                 dma, dma, dma((PLANES,)), dma((DEEP,)), dma((PLANES,)), dma((DEEP,)),
                 dma((DEEP,)), dma((DEEP, ORB)), dma((DEEP,)), dma((DEEP, ORB, SIDE - 1)), dma((DEEP, ORB)), dma((DEEP, ORB)),
                 dma, dma, dma((3, DEEP)), dma((3, WORK)), dma((2,)), dma((2,)), dma((2,)), dma((2,)),
                 dma((4,)), pltpu.SemaphoreType.REGULAR,
             ],
             compiler_params=pltpu.CompilerParams(
-                collective_id=0, has_side_effects=True, vmem_limit_bytes=48 * 1024 * 1024
+                collective_id=0, has_side_effects=True, vmem_limit_bytes=(64 << 20) - (1 << 19)
             ),
         )(block_list, coupling, left_edge, shard, right_env[0], start)
-        return env[None], jnp.swapaxes(state, 1, 2)[None], energy[0, 0:1]
+        return env[None], jnp.swapaxes(state, 1, 2)[None], energy.reshape(1)
 
     in_specs = (
         P("term", None, None, None),

time: 151 us -> 142 us (0.940)
  Pallas kernels: 144 us -> 135 us
  local copies, waits for them, and re-layouts: 6.18 us -> 3.85 us
  between operations: 0.66 us -> 2.34 us
    pallas_call x1, Pallas kernels: 144 us -> 135 us  [body(): pl.pallas_call(functools.partial(kernel, sites, terms), out_shape=(jax.Sh...]
    unnamed x15 -> x7, local copies, waits for them, and re-layouts: 5.66 us -> 3.85 us
where the time goes in v3:
time: 142 us; the launch traced here: 141 us
  Pallas kernels  135 us (95%)
  local copies, waits for them, and re-layouts  3.85 us (3%)
  between operations  2.34 us (2%)
    pallas_call x1, Pallas kernels, body(): pl.pallas_call(functools.partial(kernel, sites, terms), out_shape=(jax.Sh...  135 us
    unnamed x7, local copies, waits for them, and re-layouts  3.85 us

profile of v3, /device:TPU:481, one launch (start us, length us, event | category | flops | bytes accessed | tf_op | source)
XLA Modules:
  0.0 141.4 jit_solution(5059098511199155227)
XLA Ops:
  0.6 0.0 copy-start
  0.6 0.7 copy-done
  1.3 0.7 copy.9.perm_ref
  2.0 135.2 %shard_map.85 = (f32[4,2,128,128]{3,2,1,0:T(8,128)}, f32[2,4,128]{2,1,0:T(4,128)}, f32[1,1]{1,0:T(1,128)}) custom-call(s32[4,4,2]{2,1,0:T(4,128)} %copy.9.perm_ref, f32[4,4,4]{2,1,0:T(4,128)} %coup_ref.1, f32[4,2,128,128]{3,2,1,0:T(8,128)} %left_ref.1, f32[32,4,128]{2,1,0:T(4,128)} %bitcast.14, f32[4,2,128,128]{3,2,1,0:T(8,128)} %bitcast.12, ...), custom_call_target="tpu_custom_call" | custom-call | tf_op jit(solution)/shard_map/pallas_call | solution.py:625
  137.2 0.0 copy-start.1
  137.2 1.9 %copy.13 = f32[1,4,2,128,128]{4,3,2,1,0:T(8,128)} copy(f32[1,4,2,128,128]{4,3,2,1,0:T(8,128)} %bitcast.13) | data formatting | bytes 1048576
  139.1 0.0 copy-done.1
  139.1 0.6 copy.14
Async XLA Ops:
  0.6 0.7 copy-start
  137.2 1.9 %copy-start.1 = (f32[2,4,128]{2,1,0:T(4,128)S(1)}, f32[2,4,128]{2,1,0:T(4,128)}, u32[]{:S(2)}) copy-start(f32[2,4,128]{2,1,0:T(4,128)} %get-tuple-element.7) | copy-start | bytes 12292

commit v4 on v3

--- a/solution.py
+++ b/solution.py
@@ -16,7 +16,7 @@
 SEC = 2
 WORK = 4
 PLANES = 4
-GROUPS = ((0, 3, 0, 4), (3, 3, 3, 6), (6, 4, 4, 7), (10, 6, 6, 9))
+GROUPS = ((0, 3, 0, 4), (3, 3, 3, 7), (6, 4, 4, 8), (10, 6, 6, 10))
 DEEP = max(group[1] for group in GROUPS)
 SIDE = 4
 MESH = pl.DeviceIdType.MESH
@@ -96,6 +96,7 @@
     full,
     starts,
     weights_b,
+    scales,
     weights_t,
     enter_hl,
     right_hl,
@@ -317,12 +318,6 @@
                 arrived(turn(i - 3), o, o % 2)
                 forward(turn(i - 3), o).start()
 
-    def gather_loop(i, carry):
-        gather_step(i)
-        return carry
-
-    lax.fori_loop(0, steps, gather_loop, 0)
-
     vec_source = slab.at[pl.ds(32, SEC)]
 
     def side_work():
@@ -349,7 +344,6 @@
 
         lax.fori_loop(0, WORK, prepare_right, 0)
 
-    pl.when(ready > 0)(side_work)
 
     def coefficient(q, index):
         return coefs[q, pl.ds(index, 1)]
@@ -362,15 +356,21 @@
         pltpu.make_async_copy(there, there, fwd_rs.at[q, o]).wait()
         for p in range(PHYS):
             root = coefficient(q, (term * ORB + o) * PHYS + p)
-            blocks = [full[q, :, :, p // 2, o * 4 + (p % 2) * SEC + t].reshape(N, N) * root for t in range(SEC)]
             columns = slice(p * N, (p + 1) * N)
+            rounded, scale = [], []
             for t in range(SEC):
-                high, low = split(blocks[t])
-                weights_t[q, o, t, 0, :, columns] = high * BF16(0.5)
+                block = (full[q, :, :, p // 2, o * 4 + (p % 2) * SEC + t].reshape(N, N) * root).T
+                size = jnp.maximum(jnp.max(jnp.abs(block), axis=0, keepdims=True) * (128.0 / 255.0), 1e-30)
+                near = (block * (1.0 / size)).astype(BF16).astype(F32)
+                high, low = split((block - (near * size) * 0.5).T)
+                weights_t[q, o, t, 0, :, columns] = high
                 weights_t[q, o, t, 1, :, columns] = low
+                rounded.append(near)
+                scale.append(size)
             source_of_first = sector(q, o, p, 0)
             for s in range(SEC):
-                weights_b[q, o, s, :, columns] = jnp.where(source_of_first == s, blocks[0], blocks[1]).T.astype(BF16)
+                weights_b[q, o, s, :, columns] = jnp.where(source_of_first == s, rounded[0], rounded[1]).astype(BF16)
+                scales[q, o, s, 0:1, columns] = jnp.where(source_of_first == s, scale[0], scale[1])
 
     def orbital(q, o):
         sides = [jnp.concatenate(split(cur[s]), axis=1) for s in range(SEC)]
@@ -378,7 +378,12 @@
         moved = []
         for pair_columns in pairs:
             blocks = [weights_b[q, o, s, :, pair_columns] for s in range(SEC)]
-            moved.append([dot(sides[s], jnp.concatenate([blocks[s], blocks[s]], axis=0)) for s in range(SEC)])
+            moved.append(
+                [
+                    dot(sides[s], jnp.concatenate([blocks[s], blocks[s]], axis=0)) * scales[q, o, s, 0:1, pair_columns]
+                    for s in range(SEC)
+                ]
+            )
         totals = [None] * SEC
         for g, pair_columns in enumerate(pairs):
             for t in range(SEC):
@@ -435,11 +440,18 @@
     def results(q, start):
         pl.when(first + q != site)(lambda: act(message(2, term, q, first + q), start))
 
-    def early(index, carry):
-        prepare(turn(index // ORB), index % ORB)
-        return carry
-
-    lax.fori_loop(0, ready * ORB, early, 0)
+    def gather_loop(i, carry):
+        gather_step(i)
+
+        @pl.when(jnp.logical_and(ready > 0, i >= 4))
+        def _():
+            for o in range(ORB):
+                prepare(turn(i - 4), o)
+
+        pl.when(jnp.logical_and(ready > 0, i == 2))(side_work)
+        return carry
+
+    lax.fori_loop(0, steps, gather_loop, 0)
     loads[2].wait()
     pl.semaphore_wait(answered, greeted(answers))
 
@@ -646,6 +658,7 @@
                 pltpu.VMEM((DEEP, SIDE, SIDE, 2, 16, 8, N), F32),
                 pltpu.VMEM((chips, SEC, 8, N), F32),
                 pltpu.VMEM((DEEP, ORB, SEC, N, PHYS * N), BF16),
+                pltpu.VMEM((DEEP, ORB, SEC, 8, PHYS * N), F32),
                 pltpu.VMEM((DEEP, ORB, SEC, 2, N, PHYS * N), BF16),
                 pltpu.VMEM((SEC, WORK * N, 2 * N), BF16),
                 pltpu.VMEM((SEC, WORK * N, 2 * N), BF16),

time: 142 us -> 142 us (level)
  no operation moved by 1% of the time
where the time goes in v4:
time: 142 us
  Pallas kernels  136 us (96%)
  local copies, waits for them, and re-layouts  3.85 us (3%)
  between operations  2.34 us (2%)
    pallas_call x1, Pallas kernels, body(): pl.pallas_call(functools.partial(kernel, sites, terms), out_shape=(jax.Sh...  136 us
    unnamed x7, local copies, waits for them, and re-layouts  3.85 us

profile of v4, /device:TPU:481, one launch (start us, length us, event | category | flops | bytes accessed | tf_op | source)
XLA Modules:
  0.0 141.8 jit_solution(8349597654773319716)
XLA Ops:
  0.6 0.0 copy-start
  0.6 0.7 copy-done
  1.3 0.7 copy.9.perm_ref
  2.0 135.7 %shard_map.85 = (f32[4,2,128,128]{3,2,1,0:T(8,128)}, f32[2,4,128]{2,1,0:T(4,128)}, f32[1,1]{1,0:T(1,128)}) custom-call(s32[4,4,2]{2,1,0:T(4,128)} %copy.9.perm_ref, f32[4,4,4]{2,1,0:T(4,128)} %coup_ref.1, f32[4,2,128,128]{3,2,1,0:T(8,128)} %left_ref.1, f32[32,4,128]{2,1,0:T(4,128)} %bitcast.14, f32[4,2,128,128]{3,2,1,0:T(8,128)} %bitcast.12, ...), custom_call_target="tpu_custom_call" | custom-call | tf_op jit(solution)/shard_map/pallas_call | solution.py:637
  137.7 0.0 copy-start.1
  137.7 1.9 %copy.13 = f32[1,4,2,128,128]{4,3,2,1,0:T(8,128)} copy(f32[1,4,2,128,128]{4,3,2,1,0:T(8,128)} %bitcast.13) | data formatting | bytes 1048576
  139.6 0.0 copy-done.1
  139.6 0.6 copy.14
Async XLA Ops:
  0.6 0.7 copy-start
  137.7 1.9 %copy-start.1 = (f32[2,4,128]{2,1,0:T(4,128)S(1)}, f32[2,4,128]{2,1,0:T(4,128)}, u32[]{:S(2)}) copy-start(f32[2,4,128]{2,1,0:T(4,128)} %get-tuple-element.7) | copy-start | bytes 12292

commit v5 on v4

--- a/solution.py
+++ b/solution.py
@@ -527,9 +527,24 @@
         (lax.rem(y + a, SIDE) * SIDE + lax.rem(x + b, SIDE)) * 2 + (core if c == 0 else 1 - core) for a, b, c in offsets
     ]
 
+    def owners_in(rows):
+        return [
+            (r * SIDE + lax.rem(x + b, SIDE)) * 2 + c
+            for r in rows
+            for b in (2, 1, 3, 0)
+            for c in (core, 1 - core)
+        ]
+
+    beside = y + 1 - 2 * (y % 2)
+    across = [lax.rem(y + 2, SIDE), lax.rem(beside + 2, SIDE)]
+    near_sector = y // 2
+    itself = 2 * SIDE + 6
+    own_half = owners_in([beside, y])
+    halves = ((1 - near_sector, owners_in(across)), (near_sector, own_half[:itself] + own_half[itself + 1 :]))
+
     def iteration(it, carry):
         slot = lax.rem(it, 2)
-        for s in range(SEC):
+        for s, owners in halves:
             high, low = split(vec[s])
             sides = jnp.concatenate(
                 [jnp.concatenate([high, low], axis=1), jnp.concatenate([high, jnp.zeros_like(high)], axis=1)], axis=0
@@ -543,14 +558,13 @@
             total = wide[:, :N] + wide[:, N:] + dot(low, enter_hl[s, :, 0:N])
             part[slot, pl.ds(s * (N // 8), N // 8)] = total.reshape(N // 8, 8, N)
 
+            for peer in owners:
+                pltpu.make_async_remote_copy(
+                    src_ref=part.at[slot, peer], dst_ref=pieces.at[slot, me], send_sem=red_ss.at[slot],
+                    recv_sem=red_rs.at[slot], device_id={"term": peer}, device_id_type=MESH,
+                ).start()
+
         pltpu.make_async_copy(part.at[slot, me], pieces.at[slot, me], red_rs.at[slot]).start()
-
-        for peer in far_first:
-            pltpu.make_async_remote_copy(
-                src_ref=part.at[slot, peer], dst_ref=pieces.at[slot, me], send_sem=red_ss.at[slot],
-                recv_sem=red_rs.at[slot], device_id={"term": peer}, device_id_type=MESH,
-            ).start()
-
         old = vec[...]
         square = total_of(old * old)
 

time: 142 us -> 141 us (level)
  no operation moved by 1% of the time
where the time goes in v5:
time: 141 us
  Pallas kernels  135 us (96%)
  local copies, waits for them, and re-layouts  3.85 us (3%)
  between operations  2.34 us (2%)
    pallas_call x1, Pallas kernels, body(): pl.pallas_call(functools.partial(kernel, sites, terms), out_shape=(jax.Sh...  135 us
    unnamed x7, local copies, waits for them, and re-layouts  3.85 us

profile of v5, /device:TPU:481, one launch (start us, length us, event | category | flops | bytes accessed | tf_op | source)
XLA Modules:
  0.0 140.9 jit_solution(125109300962404151)
XLA Ops:
  0.6 0.0 copy-start
  0.6 0.7 copy-done
  1.3 0.7 copy.9.perm_ref
  2.0 134.7 %shard_map.85 = (f32[4,2,128,128]{3,2,1,0:T(8,128)}, f32[2,4,128]{2,1,0:T(4,128)}, f32[1,1]{1,0:T(1,128)}) custom-call(s32[4,4,2]{2,1,0:T(4,128)} %copy.9.perm_ref, f32[4,4,4]{2,1,0:T(4,128)} %coup_ref.1, f32[4,2,128,128]{3,2,1,0:T(8,128)} %left_ref.1, f32[32,4,128]{2,1,0:T(4,128)} %bitcast.14, f32[4,2,128,128]{3,2,1,0:T(8,128)} %bitcast.12, ...), custom_call_target="tpu_custom_call" | custom-call | tf_op jit(solution)/shard_map/pallas_call | solution.py:651
  136.7 0.0 copy-start.1
  136.7 1.9 %copy.13 = f32[1,4,2,128,128]{4,3,2,1,0:T(8,128)} copy(f32[1,4,2,128,128]{4,3,2,1,0:T(8,128)} %bitcast.13) | data formatting | bytes 1048576
  138.6 0.0 copy-done.1
  138.6 0.6 copy.14
Async XLA Ops:
  0.6 0.7 copy-start
  136.7 1.9 %copy-start.1 = (f32[2,4,128]{2,1,0:T(4,128)S(1)}, f32[2,4,128]{2,1,0:T(4,128)}, u32[]{:S(2)}) copy-start(f32[2,4,128]{2,1,0:T(4,128)} %get-tuple-element.7) | copy-start | bytes 12292

commit v6 on v5

--- a/solution.py
+++ b/solution.py
@@ -542,6 +542,14 @@
     own_half = owners_in([beside, y])
     halves = ((1 - near_sector, owners_in(across)), (near_sector, own_half[:itself] + own_half[itself + 1 :]))
 
+    def leaving(w, carry):
+        @pl.when(first_plane(site) + w != site)
+        def _():
+            received(2, w)
+            env_ref[w, 0], env_ref[w, 1] = unpack(2, w)
+
+        return carry
+
     def iteration(it, carry):
         slot = lax.rem(it, 2)
         for s, owners in halves:
@@ -567,6 +575,7 @@
         pltpu.make_async_copy(part.at[slot, me], pieces.at[slot, me], red_rs.at[slot]).start()
         old = vec[...]
         square = total_of(old * old)
+        leaving(lax.rem(it + WORK - 1, WORK), 0)
 
         pltpu.make_async_copy(pieces.at[slot], pieces.at[slot], red_rs.at[slot]).wait()
         reduced[slot] = jnp.sum(pieces[slot], axis=0) * (1.0 / (WORK * terms))
@@ -595,16 +604,6 @@
     for s in range(SEC):
         rows = vec[s, pl.ds(pl.multiple_of(chip * 8, 8), 8)]
         state_ref[s] = jnp.where(core == 0, rows[0:4], rows[4:8])
-
-    def leaving(w, carry):
-        @pl.when(first_plane(site) + w != site)
-        def _():
-            received(2, w)
-            env_ref[w, 0], env_ref[w, 1] = unpack(2, w)
-
-        return carry
-
-    lax.fori_loop(0, WORK, leaving, 0)
 
     def slab_done(r, carry):
         @pl.when(to_base + r != site)

time: 141 us -> 143 us (1.014); the launches traced: 141 us -> 141 us
  no operation moved by 1% of the time
where the time goes in v6:
time: 143 us; the launch traced here: 141 us
  Pallas kernels  134 us (94%)
  local copies, waits for them, and re-layouts  3.85 us (3%)
  between operations  2.34 us (2%)
    pallas_call x1, Pallas kernels, body(): pl.pallas_call(functools.partial(kernel, sites, terms), out_shape=(jax.Sh...  134 us
    unnamed x7, local copies, waits for them, and re-layouts  3.85 us

profile of v6, /device:TPU:481, one launch (start us, length us, event | category | flops | bytes accessed | tf_op | source)
XLA Modules:
  0.0 140.5 jit_solution(2494952336042491136)
XLA Ops:
  0.6 0.0 copy-start
  0.6 0.7 copy-done
  1.3 0.7 copy.9.perm_ref
  2.0 134.3 %shard_map.85 = (f32[4,2,128,128]{3,2,1,0:T(8,128)}, f32[2,4,128]{2,1,0:T(4,128)}, f32[1,1]{1,0:T(1,128)}) custom-call(s32[4,4,2]{2,1,0:T(4,128)} %copy.9.perm_ref, f32[4,4,4]{2,1,0:T(4,128)} %coup_ref.1, f32[4,2,128,128]{3,2,1,0:T(8,128)} %left_ref.1, f32[32,4,128]{2,1,0:T(4,128)} %bitcast.14, f32[4,2,128,128]{3,2,1,0:T(8,128)} %bitcast.12, ...), custom_call_target="tpu_custom_call" | custom-call | tf_op jit(solution)/shard_map/pallas_call | solution.py:650
  136.4 0.0 copy-start.1
  136.4 1.9 %copy.13 = f32[1,4,2,128,128]{4,3,2,1,0:T(8,128)} copy(f32[1,4,2,128,128]{4,3,2,1,0:T(8,128)} %bitcast.13) | data formatting | bytes 1048576
  138.2 0.0 copy-done.1
  138.2 0.6 copy.14
Async XLA Ops:
  0.6 0.7 copy-start
  136.4 1.9 %copy-start.1 = (f32[2,4,128]{2,1,0:T(4,128)S(1)}, f32[2,4,128]{2,1,0:T(4,128)}, u32[]{:S(2)}) copy-start(f32[2,4,128]{2,1,0:T(4,128)} %get-tuple-element.7) | copy-start | bytes 12292
